TPU v7x, 512 devices: a whole 4x4x16 slice. The times are simulated.
512 devices in a mesh: blk: 32 (over x_hi, z), aux: 16 (over x_lo, y, core).
Axes of the slice: x: 4 (x_hi: 2, x_lo: 2; x = x_hi * 2 + x_lo), y: 4, z: 16, core: 2. Of those that a mesh axis runs over, the one named last changes fastest.
Arguments:
- tensor: bfloat16 [16, 64, 3, 128, 128], P('aux', 'blk'), may hold values from -0.25 to 0.25
- intersection: int32 [64, 2], P('blk'), may hold values 0 or 1
- counts: int32 [64], replicated, may hold values from 64 to 128
- d_occ: bfloat16 [64, 5, 128, 128], P('blk'), as said below
- d_virt: bfloat16 [64, 5, 128, 128], P('blk'), as said below
Outputs:
- response: float32 [16, 16], P('aux')
Inputs may be any that keep to these rules, and one draw needn't show every extreme that they name: d_occ and d_virt are symmetric: block v of row block m is the transpose of block 4 - v of row block (m + v - 2) mod 64. `d_virt`: symmetric in the same way as d_occ.
All inputs are finite; a program needn't handle non-finite values. No bound on the sum of `intersection` on one device may be relied on, other than what follows from the above.
Results may differ from a plain program's by a relative error of at most 0.0028.
Values may be sent and summed in bfloat16 or wider, within the bound.
A program may use at most 64 MiB of HBM per device.

v0:
```python
import functools

import jax
import jax.numpy as jnp
from jax import lax
from jax.experimental import pallas as pl
from jax.experimental.pallas import tpu as pltpu
from jax.sharding import PartitionSpec as P

MESH = pl.DeviceIdType.MESH
BS = 128
PACK = 16


def kernel(
    n_blk,
    n_aux,
    inter_hbm,
    counts_hbm,
    tensor_ref,
    docc_ref,
    dvirt_ref,
    out_ref,
    inter_ref,
    counts_ref,
    raw,
    omat,
    dmat,
    corner,
    ball,
    w_own,
    all_b,
    all_w,
    row_out,
    row_in,
    sum_out,
    sum_in,
    load_sem,
    rim_send,
    rim_recv,
    a2a_send,
    a2a_recv,
    known,
):
    b = lax.axis_index("blk")
    q = lax.axis_index("aux")
    nblocks = counts_ref.shape[0]
    rows = raw.shape[0]
    share = rows // n_aux
    team = n_aux // 2
    strip = 3 * BS // team
    seat = lax.rem(q, team)
    left = lax.rem(b + n_blk - 1, n_blk)
    right = lax.rem(b + 1, n_blk)
    own = ball.at[pl.ds(rows, rows)]

    def tile(ref, i, j):
        return ref.at[
            pl.ds(pl.multiple_of(i * BS, BS), BS), pl.ds(pl.multiple_of(j * BS, BS), BS)
        ]

    barrier = pltpu.get_barrier_semaphore()

    def greet_blk(i, carry):
        there = lax.rem(b + i, n_blk)
        pl.semaphore_signal(barrier, inc=1, device_id={"blk": there}, device_id_type=MESH)
        return carry

    def greet_aux(i, carry):
        there = lax.rem(q + i, n_aux)
        pl.semaphore_signal(barrier, inc=1, device_id={"aux": there}, device_id_type=MESH)
        return carry

    loads = [
        pltpu.make_async_copy(tensor_ref, raw, load_sem.at[0]),
        pltpu.make_async_copy(inter_hbm, inter_ref, load_sem.at[3]),
        pltpu.make_async_copy(counts_hbm, counts_ref, load_sem.at[4]),
    ]
    for load in loads:
        load.start()

    def stored(ref, m, v):
        return ref.at[pl.ds((5 * m + v) * BS, BS)]

    for m in range(2):
        for c in range(4):
            pltpu.make_async_copy(
                stored(dvirt_ref, m, c + 1 - m), tile(dmat, 3 + m, c), load_sem.at[1]
            ).start()
        pltpu.make_async_copy(stored(dvirt_ref, m, 4 * m), corner.at[m], load_sem.at[1]).start()
        for v in range(5):
            pltpu.make_async_copy(
                stored(docc_ref, m, v), tile(omat, m, m + v), load_sem.at[2]
            ).start()

    greet_blk(1, 0)
    greet_blk(n_blk - 1, 0)
    lax.fori_loop(1, n_aux, greet_aux, 0)

    zero = jnp.zeros((BS, BS), jnp.bfloat16)
    for c in range(4):
        for r in range(8):
            if not 0 <= r - c <= 4:
                tile(dmat, r, c)[...] = zero
    for m in range(2):
        tile(omat, m, 5 - 5 * m)[...] = zero

    for load in loads:
        load.wait()
    row_ids = lax.broadcasted_iota(jnp.int32, (BS, BS), 0)
    col_ids = lax.broadcasted_iota(jnp.int32, (BS, BS), 1)

    for m in range(2):
        row = 2 * b + m
        own_count = counts_ref[row]
        for w in range(3):
            col_count = counts_ref[lax.rem(row + w - 1 + nblocks, nblocks)]
            if w != 1:
                col_count = col_count * inter_ref[m, w // 2]
            keep = (row_ids < own_count) & (col_ids < col_count)
            at = pl.ds((m * 3 + w) * BS, BS)
            block = jnp.where(keep, raw[at, :].astype(jnp.float32), 0.0)
            own[at, :] = block.astype(jnp.bfloat16)

    pltpu.make_async_copy(dvirt_ref, dvirt_ref, load_sem.at[1]).wait()

    def turn(block):
        return block[...].astype(jnp.float32).T.astype(jnp.bfloat16)

    tile(dmat, 1, 1)[...] = turn(corner.at[0])
    tile(dmat, 2, 1)[...] = turn(tile(dmat, 3, 0))
    tile(dmat, 5, 1)[...] = turn(tile(dmat, 3, 3))
    tile(dmat, 2, 2)[...] = turn(tile(dmat, 4, 0))
    tile(dmat, 5, 2)[...] = turn(tile(dmat, 4, 3))
    tile(dmat, 6, 2)[...] = turn(corner.at[1])
    pl.semaphore_wait(barrier, 2 + n_aux - 1)

    def tell(step):
        if step < known.shape[0]:
            for there in (b + 2**step, b + n_blk - 2**step):
                pl.semaphore_signal(
                    known.at[step],
                    inc=1,
                    device_id={"blk": lax.rem(there, n_blk)},
                    device_id_type=MESH,
                )

    def learn(step):
        if step < known.shape[0]:
            pl.semaphore_wait(known.at[step], 2)

    def to_blk(src, dst, sem, there):
        return pltpu.make_async_remote_copy(
            src_ref=src,
            dst_ref=dst,
            send_sem=rim_send.at[sem],
            recv_sem=rim_recv.at[sem],
            device_id={"blk": there},
            device_id_type=MESH,
        )

    def band(r, c):
        return dmat.at[
            pl.ds(pl.multiple_of(r * BS + seat * strip, PACK), strip), pl.ds(c * BS, BS)
        ]

    rims = [
        to_blk(band(2, 2), band(0, 0), 0, right),
        to_blk(band(3, 1), band(5, 3), 1, left),
        to_blk(own, ball.at[pl.ds(0, rows)], 2, right),
        to_blk(own, ball.at[pl.ds(2 * rows, rows)], 3, left),
    ]
    for rim in rims:
        rim.start()
    tell(0)

    def scatter(src, first, dst, sem):
        def piece(there):
            return src.at[pl.ds(pl.multiple_of(first + there * share, PACK), share)]

        def send(i, carry):
            there = lax.rem(q + i, n_aux)
            pltpu.make_async_remote_copy(
                src_ref=piece(there),
                dst_ref=dst.at[q],
                send_sem=a2a_send.at[sem],
                recv_sem=a2a_recv.at[sem],
                device_id={"aux": there},
                device_id_type=MESH,
            ).start()
            return carry

        lax.fori_loop(1, n_aux, send, 0)
        dst[q] = piece(q)[...]

    def scattered(dst, sem):
        pltpu.make_async_copy(
            dst.at[pl.ds(0, n_aux - 1)], dst.at[pl.ds(0, n_aux - 1)], sem
        ).wait()

    scatter(ball, rows, all_b, 0)

    def hand(i, carry):
        there = q - seat + lax.rem(seat + i, team)
        for r, c in ((0, 0), (5, 3)):
            pltpu.make_async_remote_copy(
                src_ref=band(r, c),
                dst_ref=band(r, c),
                send_sem=a2a_send.at[4],
                recv_sem=a2a_recv.at[4],
                device_id={"aux": there},
                device_id_type=MESH,
            ).start()
        return carry

    rims[0].wait_recv()
    rims[1].wait_recv()
    lax.fori_loop(1, team, hand, 0)
    learn(0)
    tell(1)

    pltpu.make_async_copy(docc_ref, docc_ref, load_sem.at[2]).wait()
    handed = dmat.at[pl.ds(0, (team - 1) * strip), pl.ds(0, 2 * BS)]
    pltpu.make_async_copy(handed, handed, a2a_recv.at[4]).wait()
    learn(1)
    tell(2)

    def part(pair):
        blocks = [ball[pl.ds((6 * pair + i) * BS, BS), :] for i in range(6)]
        b_pair = jnp.concatenate(
            [
                jnp.concatenate(blocks[:3] + [zero], axis=1),
                jnp.concatenate([zero] + blocks[3:], axis=1),
            ],
            axis=0,
        )
        at = pl.ds(2 * pair * BS, 4 * BS)
        x_pair = jnp.dot(b_pair, dmat[at, :], preferred_element_type=jnp.float32)
        return jnp.dot(
            omat[:, pl.ds(2 * pair * BS, 2 * BS)],
            x_pair.astype(jnp.bfloat16),
            preferred_element_type=jnp.float32,
        )

    total = part(1)
    rims[2].wait_recv()
    total = total + part(0)
    rims[3].wait_recv()
    learn(2)
    tell(3)
    total = total + part(2)
    total = total.astype(jnp.bfloat16)
    for m in range(2):
        for w in range(3):
            w_own[pl.ds((m * 3 + w) * BS, BS), :] = total[
                m * BS : (m + 1) * BS, (m + w) * BS : (m + w + 1) * BS
            ]

    scatter(w_own, 0, all_w, 1)
    scattered(all_b, a2a_recv.at[0])
    groups = range(share // PACK)
    size = n_aux * PACK

    def flat(ref):
        return jnp.concatenate(
            [ref[:, pl.ds(g * PACK, PACK), :].reshape(size, BS) for g in groups], axis=1
        )

    b_turned = flat(all_b).astype(jnp.float32).T.astype(jnp.bfloat16)
    scattered(all_w, a2a_recv.at[1])
    gram = jnp.dot(flat(all_w), b_turned, preferred_element_type=jnp.float32)
    same = (lax.broadcasted_iota(jnp.int32, (size, size), 0) & (PACK - 1)) == (
        lax.broadcasted_iota(jnp.int32, (size, size), 1) & (PACK - 1)
    )
    gram = jnp.sum(jnp.where(same, gram, 0.0).reshape(n_aux, PACK, size), axis=1)
    fold = (
        lax.broadcasted_iota(jnp.int32, (size, BS), 0) // PACK
        == lax.broadcasted_iota(jnp.int32, (size, BS), 1)
    ).astype(jnp.float32)
    gram = jnp.dot(
        gram, fold, precision=lax.Precision.HIGHEST, preferred_element_type=jnp.float32
    )
    for p in range(n_aux):
        row_out[p] = gram[p : p + 1, :]

    def send_row(i, carry):
        there = lax.rem(q + i, n_aux)
        pltpu.make_async_remote_copy(
            src_ref=row_out.at[there],
            dst_ref=row_in.at[q],
            send_sem=a2a_send.at[2],
            recv_sem=a2a_recv.at[2],
            device_id={"aux": there},
            device_id_type=MESH,
        ).start()
        return carry

    lax.fori_loop(1, n_aux, send_row, 0)
    row_in[q] = row_out[q]
    scattered(row_in, a2a_recv.at[2])
    sum_out[...] = jnp.sum(row_in[...], axis=0)
    learn(3)

    def send_sum(i, carry):
        there = lax.rem(b + i, n_blk)
        pltpu.make_async_remote_copy(
            src_ref=sum_out,
            dst_ref=sum_in.at[b],
            send_sem=a2a_send.at[3],
            recv_sem=a2a_recv.at[3],
            device_id={"blk": there},
            device_id_type=MESH,
        ).start()
        return carry

    lax.fori_loop(1, n_blk, send_sum, 0)
    sum_in[b] = sum_out[...]
    pltpu.make_async_copy(
        sum_in.at[pl.ds(0, n_blk - 1)], sum_in.at[pl.ds(0, n_blk - 1)], a2a_recv.at[3]
    ).wait()
    out_ref[...] = jnp.sum(sum_in[...], axis=0)[:, : out_ref.shape[1]]

    for rim in rims:
        rim.wait_send()
    scattered(all_b, a2a_send.at[0])
    scattered(all_w, a2a_send.at[1])
    scattered(row_in, a2a_send.at[2])
    pltpu.make_async_copy(handed, handed, a2a_send.at[4]).wait()
    pltpu.make_async_copy(
        sum_in.at[pl.ds(0, n_blk - 1)], sum_in.at[pl.ds(0, n_blk - 1)], a2a_send.at[3]
    ).wait()


def solution(mesh):
    n_blk, n_aux = mesh.shape["blk"], mesh.shape["aux"]
    rows = 2 * 3 * BS
    share = rows // n_aux
    steps = n_blk.bit_length() - 2
    hbm = pl.BlockSpec(memory_space=pltpu.HBM)

    def on_device(tensor, intersection, counts, d_occ, d_virt):
        return pl.pallas_call(
            functools.partial(kernel, n_blk, n_aux),
            out_shape=jax.ShapeDtypeStruct((1, n_aux), jnp.float32),
            in_specs=[hbm] * 5,
            out_specs=pl.BlockSpec(memory_space=pltpu.VMEM),
            scratch_shapes=[
                pltpu.SMEM(intersection.shape, jnp.int32),
                pltpu.SMEM(counts.shape, jnp.int32),
                pltpu.VMEM((rows, BS), jnp.bfloat16),
                pltpu.VMEM((2 * BS, 6 * BS), jnp.bfloat16),
                pltpu.VMEM((8 * BS, 4 * BS), jnp.bfloat16),
                pltpu.VMEM((2, BS, BS), jnp.bfloat16),
                pltpu.VMEM((3 * rows, BS), jnp.bfloat16),
                pltpu.VMEM((rows, BS), jnp.bfloat16),
                pltpu.VMEM((n_aux, share, BS), jnp.bfloat16),
                pltpu.VMEM((n_aux, share, BS), jnp.bfloat16),
                pltpu.VMEM((n_aux, 1, BS), jnp.float32),
                pltpu.VMEM((n_aux, 1, BS), jnp.float32),
                pltpu.VMEM((1, BS), jnp.float32),
                pltpu.VMEM((n_blk, 1, BS), jnp.float32),
                pltpu.SemaphoreType.DMA((5,)),
                pltpu.SemaphoreType.DMA((4,)),
                pltpu.SemaphoreType.DMA((4,)),
                pltpu.SemaphoreType.DMA((5,)),
                pltpu.SemaphoreType.DMA((5,)),
                pltpu.SemaphoreType.REGULAR((steps,)),
            ],
            compiler_params=pltpu.CompilerParams(
                collective_id=0,
                has_side_effects=True,
                vmem_limit_bytes=65536 * 1000,
            ),
        )(
            intersection,
            counts,
            tensor.reshape(rows, BS),
            d_occ.reshape(2 * 5 * BS, BS),
            d_virt.reshape(2 * 5 * BS, BS),
        )

    return jax.shard_map(
        on_device,
        mesh=mesh,
        in_specs=(
            P("aux", "blk", None, None, None),
            P("blk", None),
            P(),
            P("blk", None, None, None),
            P("blk", None, None, None),
        ),
        out_specs=P("aux", None),
        check_vma=False,
    )
```

profile of v0, /device:TPU:1, one launch (start us, length us, event | category | flops | bytes accessed | tf_op | source)
XLA Modules:
  0.0 44.5 jit_solution(2181022105550881328)
XLA Ops:
  0.0 43.3 %shard_map.55 = f32[1,16]{1,0:T(1,128)} custom-call(s32[2,2]{1,0:T(2,128)} %inter_hbm.1, s32[64]{0:T(128)} %counts_hbm.1, bf16[768,128]{1,0:T(8,128)(2,1)} %bitcast.5, bf16[1280,128]{1,0:T(8,128)(2,1)} %bitcast.3, bf16[1280,128]{1,0:T(8,128)(2,1)} %bitcast.4), custom_call_target="tpu_custom_call" | custom-call | tf_op jit(solution)/shard_map/pallas_call | solution.py:342
  43.3 1.2 %copy.7 = f32[1,16]{1,0:T(1,128)} copy(f32[1,16]{1,0:T(1,128)} %shard_map.55) | data formatting | bytes 128
where the time goes:
time: 44.7 us; the launch traced here: 44.5 us
  Pallas kernels  43.3 us (97%)
  local copies, waits for them, and re-layouts  1.19 us (3%)
    pallas_call x1, Pallas kernels, on_device(): pl.pallas_call(functools.partial(kernel, n_blk, n_aux), out_shape=jax.Sha...  43.3 us
    unnamed x1, local copies, waits for them, and re-layouts  1.19 us

commit v1 on v0

--- a/solution.py
+++ b/solution.py
@@ -28,6 +28,7 @@
     dmat,
     corner,
     ball,
+    relay,
     w_own,
     all_b,
     all_w,
@@ -41,6 +42,8 @@
     a2a_send,
     a2a_recv,
     known,
+    relay_send,
+    relay_recv,
 ):
     b = lax.axis_index("blk")
     q = lax.axis_index("aux")
@@ -54,6 +57,25 @@
     right = lax.rem(b + 1, n_blk)
     own = ball.at[pl.ds(rows, rows)]
 
+    n_z = n_blk // 2
+    z = lax.rem(b, n_z)
+    top = z == n_z - 1
+    wraps = (z == 0) | top
+    across = lax.rem(q + n_aux // 2, n_aux)
+
+    def other_half(there):
+        return lax.rem(there + n_z, n_blk)
+
+    far_side = jnp.where(top, right, left)
+    between = [
+        {"aux": across},
+        {"blk": other_half(b), "aux": across},
+    ]
+    beyond = [
+        {"blk": far_side, "aux": across},
+        {"blk": other_half(far_side), "aux": across},
+    ]
+
     def tile(ref, i, j):
         return ref.at[
             pl.ds(pl.multiple_of(i * BS, BS), BS), pl.ds(pl.multiple_of(j * BS, BS), BS)
@@ -96,6 +118,12 @@
     greet_blk(1, 0)
     greet_blk(n_blk - 1, 0)
     lax.fori_loop(1, n_aux, greet_aux, 0)
+
+    @pl.when(wraps)
+    def _():
+        for there in [between[1]] + beyond:
+            pl.semaphore_signal(barrier, inc=1, device_id=there, device_id_type=MESH)
+
 
     zero = jnp.zeros((BS, BS), jnp.bfloat16)
     for c in range(4):
@@ -133,7 +161,7 @@
     tile(dmat, 2, 2)[...] = turn(tile(dmat, 4, 0))
     tile(dmat, 5, 2)[...] = turn(tile(dmat, 4, 3))
     tile(dmat, 6, 2)[...] = turn(corner.at[1])
-    pl.semaphore_wait(barrier, 2 + n_aux - 1)
+    pl.semaphore_wait(barrier, 2 + n_aux - 1 + jnp.where(wraps, 3, 0))
 
     def tell(step):
         if step < known.shape[0]:
@@ -170,8 +198,45 @@
         to_blk(own, ball.at[pl.ds(0, rows)], 2, right),
         to_blk(own, ball.at[pl.ds(2 * rows, rows)], 3, left),
     ]
-    for rim in rims:
-        rim.start()
+    rims[0].start()
+    rims[1].start()
+    pl.when(jnp.logical_not(top))(rims[2].start)
+    pl.when(z != 0)(rims[3].start)
+    part_rows = rows // 2
+
+    def pass_on(src, dst, send, recv, there):
+        pltpu.make_async_remote_copy(
+            src_ref=src,
+            dst_ref=dst,
+            send_sem=send,
+            recv_sem=recv,
+            device_id=there,
+            device_id_type=MESH,
+        ).start()
+
+    def outward(side):
+        for k in range(2):
+            pass_on(
+                own.at[pl.ds(k * part_rows, part_rows)],
+                relay.at[k],
+                rim_send.at[side],
+                relay_recv.at[k],
+                between[k],
+            )
+
+    def onward(side):
+        for k in range(2):
+            pltpu.make_async_copy(relay.at[k], relay.at[k], relay_recv.at[k]).wait()
+            pass_on(
+                relay.at[k],
+                ball.at[pl.ds((side - 2) * 2 * rows + k * part_rows, part_rows)],
+                relay_send,
+                rim_recv.at[side],
+                beyond[k],
+            )
+
+    pl.when(top)(functools.partial(outward, 2))
+    pl.when(z == 0)(functools.partial(outward, 3))
     tell(0)
 
     def scatter(src, first, dst, sem):
@@ -197,8 +262,6 @@
         pltpu.make_async_copy(
             dst.at[pl.ds(0, n_aux - 1)], dst.at[pl.ds(0, n_aux - 1)], sem
         ).wait()
-
-    scatter(ball, rows, all_b, 0)
 
     def hand(i, carry):
         there = q - seat + lax.rem(seat + i, team)
@@ -216,6 +279,9 @@
     rims[0].wait_recv()
     rims[1].wait_recv()
     lax.fori_loop(1, team, hand, 0)
+    pl.when(top)(functools.partial(onward, 2))
+    pl.when(z == 0)(functools.partial(onward, 3))
+    scatter(ball, rows, all_b, 0)
     learn(0)
     tell(1)
 
@@ -322,6 +388,11 @@
 
     for rim in rims:
         rim.wait_send()
+
+    @pl.when(wraps)
+    def _():
+        pltpu.make_async_copy(relay, relay, relay_send).wait()
+
     scattered(all_b, a2a_send.at[0])
     scattered(all_w, a2a_send.at[1])
     scattered(row_in, a2a_send.at[2])
@@ -352,6 +423,7 @@
                 pltpu.VMEM((8 * BS, 4 * BS), jnp.bfloat16),
                 pltpu.VMEM((2, BS, BS), jnp.bfloat16),
                 pltpu.VMEM((3 * rows, BS), jnp.bfloat16),
+                pltpu.VMEM((2, rows // 2, BS), jnp.bfloat16),
                 pltpu.VMEM((rows, BS), jnp.bfloat16),
                 pltpu.VMEM((n_aux, share, BS), jnp.bfloat16),
                 pltpu.VMEM((n_aux, share, BS), jnp.bfloat16),
@@ -365,6 +437,8 @@
                 pltpu.SemaphoreType.DMA((5,)),
                 pltpu.SemaphoreType.DMA((5,)),
                 pltpu.SemaphoreType.REGULAR((steps,)),
+                pltpu.SemaphoreType.DMA,
+                pltpu.SemaphoreType.DMA((2,)),
             ],
             compiler_params=pltpu.CompilerParams(
                 collective_id=0,

time: 44.7 us -> 45.4 us (1.016)
  Pallas kernels: 43.3 us -> 44 us
    pallas_call x1, Pallas kernels: 43.3 us -> 44 us  [on_device(): pl.pallas_call(functools.partial(kernel, n_blk, n_aux), out_shape=jax.Sha...]
where the time goes in v1:
time: 45.4 us; the launch traced here: 45.2 us
  Pallas kernels  44 us (97%)
  local copies, waits for them, and re-layouts  1.19 us (3%)
    pallas_call x1, Pallas kernels, on_device(): pl.pallas_call(functools.partial(kernel, n_blk, n_aux), out_shape=jax.Sha...  44 us
    unnamed x1, local copies, waits for them, and re-layouts  1.19 us

profile of v1, /device:TPU:1, one launch (start us, length us, event | category | flops | bytes accessed | tf_op | source)
XLA Modules:
  0.0 45.2 jit_solution(14798608822786045443)
XLA Ops:
  0.0 44.0 %shard_map.55 = f32[1,16]{1,0:T(1,128)} custom-call(s32[2,2]{1,0:T(2,128)} %inter_hbm.1, s32[64]{0:T(128)} %counts_hbm.1, bf16[768,128]{1,0:T(8,128)(2,1)} %bitcast.5, bf16[1280,128]{1,0:T(8,128)(2,1)} %bitcast.3, bf16[1280,128]{1,0:T(8,128)(2,1)} %bitcast.4), custom_call_target="tpu_custom_call" | custom-call | tf_op jit(solution)/shard_map/pallas_call | solution.py:413
  44.0 1.2 %copy.7 = f32[1,16]{1,0:T(1,128)} copy(f32[1,16]{1,0:T(1,128)} %shard_map.55) | data formatting | bytes 128

commit v2 on v0

--- a/solution.py
+++ b/solution.py
@@ -47,9 +47,6 @@
     nblocks = counts_ref.shape[0]
     rows = raw.shape[0]
     share = rows // n_aux
-    team = n_aux // 2
-    strip = 3 * BS // team
-    seat = lax.rem(q, team)
     left = lax.rem(b + n_blk - 1, n_blk)
     right = lax.rem(b + 1, n_blk)
     own = ball.at[pl.ds(rows, rows)]
@@ -160,9 +157,7 @@
         )
 
     def band(r, c):
-        return dmat.at[
-            pl.ds(pl.multiple_of(r * BS + seat * strip, PACK), strip), pl.ds(c * BS, BS)
-        ]
+        return dmat.at[pl.ds(r * BS, 3 * BS), pl.ds(c * BS, BS)]
 
     rims = [
         to_blk(band(2, 2), band(0, 0), 0, right),
@@ -200,28 +195,12 @@
 
     scatter(ball, rows, all_b, 0)
 
-    def hand(i, carry):
-        there = q - seat + lax.rem(seat + i, team)
-        for r, c in ((0, 0), (5, 3)):
-            pltpu.make_async_remote_copy(
-                src_ref=band(r, c),
-                dst_ref=band(r, c),
-                send_sem=a2a_send.at[4],
-                recv_sem=a2a_recv.at[4],
-                device_id={"aux": there},
-                device_id_type=MESH,
-            ).start()
-        return carry
-
+    learn(0)
+    tell(1)
+
+    pltpu.make_async_copy(docc_ref, docc_ref, load_sem.at[2]).wait()
     rims[0].wait_recv()
     rims[1].wait_recv()
-    lax.fori_loop(1, team, hand, 0)
-    learn(0)
-    tell(1)
-
-    pltpu.make_async_copy(docc_ref, docc_ref, load_sem.at[2]).wait()
-    handed = dmat.at[pl.ds(0, (team - 1) * strip), pl.ds(0, 2 * BS)]
-    pltpu.make_async_copy(handed, handed, a2a_recv.at[4]).wait()
     learn(1)
     tell(2)
 
@@ -266,20 +245,26 @@
             [ref[:, pl.ds(g * PACK, PACK), :].reshape(size, BS) for g in groups], axis=1
         )
 
-    b_turned = flat(all_b).astype(jnp.float32).T.astype(jnp.bfloat16)
+    b_turned = (
+        jnp.swapaxes(flat(all_b).astype(jnp.float32).reshape(n_aux, PACK, share // PACK * BS), 0, 1)
+        .reshape(size, share // PACK * BS)
+        .T.astype(jnp.bfloat16)
+    )
     scattered(all_w, a2a_recv.at[1])
     gram = jnp.dot(flat(all_w), b_turned, preferred_element_type=jnp.float32)
     same = (lax.broadcasted_iota(jnp.int32, (size, size), 0) & (PACK - 1)) == (
-        lax.broadcasted_iota(jnp.int32, (size, size), 1) & (PACK - 1)
+        lax.broadcasted_iota(jnp.int32, (size, size), 1) // n_aux
     )
-    gram = jnp.sum(jnp.where(same, gram, 0.0).reshape(n_aux, PACK, size), axis=1)
-    fold = (
-        lax.broadcasted_iota(jnp.int32, (size, BS), 0) // PACK
-        == lax.broadcasted_iota(jnp.int32, (size, BS), 1)
-    ).astype(jnp.float32)
-    gram = jnp.dot(
-        gram, fold, precision=lax.Precision.HIGHEST, preferred_element_type=jnp.float32
-    )
+    gram = jnp.where(same, gram, 0.0)
+    lanes = min(size, BS)
+    gram = functools.reduce(jnp.add, [gram[:, c : c + lanes] for c in range(0, size, lanes)])
+    gram = jnp.sum(gram.reshape(n_aux, PACK, lanes), axis=1)
+    turn_by = lanes // 2
+    while turn_by >= n_aux:
+        gram = gram + pltpu.roll(gram, turn_by, 1)
+        turn_by //= 2
+    if lanes < BS:
+        gram = jnp.concatenate([gram] * (BS // lanes), axis=1)
     for p in range(n_aux):
         row_out[p] = gram[p : p + 1, :]
 
@@ -302,18 +287,22 @@
     learn(3)
 
     def send_sum(i, carry):
-        there = lax.rem(b + i, n_blk)
-        pltpu.make_async_remote_copy(
-            src_ref=sum_out,
-            dst_ref=sum_in.at[b],
-            send_sem=a2a_send.at[3],
-            recv_sem=a2a_recv.at[3],
-            device_id={"blk": there},
-            device_id_type=MESH,
-        ).start()
+        there = lax.rem(i, 2) * (n_blk // 2) + i // 2
+
+        @pl.when(there != b)
+        def _():
+            pltpu.make_async_remote_copy(
+                src_ref=sum_out,
+                dst_ref=sum_in.at[b],
+                send_sem=a2a_send.at[3],
+                recv_sem=a2a_recv.at[3],
+                device_id={"blk": there},
+                device_id_type=MESH,
+            ).start()
+
         return carry
 
-    lax.fori_loop(1, n_blk, send_sum, 0)
+    lax.fori_loop(0, n_blk, send_sum, 0)
     sum_in[b] = sum_out[...]
     pltpu.make_async_copy(
         sum_in.at[pl.ds(0, n_blk - 1)], sum_in.at[pl.ds(0, n_blk - 1)], a2a_recv.at[3]
@@ -325,7 +314,6 @@
     scattered(all_b, a2a_send.at[0])
     scattered(all_w, a2a_send.at[1])
     scattered(row_in, a2a_send.at[2])
-    pltpu.make_async_copy(handed, handed, a2a_send.at[4]).wait()
     pltpu.make_async_copy(
         sum_in.at[pl.ds(0, n_blk - 1)], sum_in.at[pl.ds(0, n_blk - 1)], a2a_send.at[3]
     ).wait()

time: 44.7 us -> 42.4 us (0.949)
  Pallas kernels: 43.3 us -> 41 us
    pallas_call x1, Pallas kernels: 43.3 us -> 41 us  [on_device(): pl.pallas_call(functools.partial(kernel, n_blk, n_aux), out_shape=jax.Sha...]
where the time goes in v2:
time: 42.4 us; the launch traced here: 42.2 us
  Pallas kernels  41 us (97%)
  local copies, waits for them, and re-layouts  1.19 us (3%)
    pallas_call x1, Pallas kernels, on_device(): pl.pallas_call(functools.partial(kernel, n_blk, n_aux), out_shape=jax.Sha...  41 us
    unnamed x1, local copies, waits for them, and re-layouts  1.19 us

profile of v2, /device:TPU:1, one launch (start us, length us, event | category | flops | bytes accessed | tf_op | source)
XLA Modules:
  0.0 42.2 jit_solution(9930678791526918970)
XLA Ops:
  0.0 41.0 %shard_map.55 = f32[1,16]{1,0:T(1,128)} custom-call(s32[2,2]{1,0:T(2,128)} %inter_hbm.1, s32[64]{0:T(128)} %counts_hbm.1, bf16[768,128]{1,0:T(8,128)(2,1)} %bitcast.5, bf16[1280,128]{1,0:T(8,128)(2,1)} %bitcast.3, bf16[1280,128]{1,0:T(8,128)(2,1)} %bitcast.4), custom_call_target="tpu_custom_call" | custom-call | tf_op jit(solution)/shard_map/pallas_call | solution.py:330
  41.0 1.2 %copy.7 = f32[1,16]{1,0:T(1,128)} copy(f32[1,16]{1,0:T(1,128)} %shard_map.55) | data formatting | bytes 128

commit v3 on v2

--- a/solution.py
+++ b/solution.py
@@ -51,11 +51,6 @@
     right = lax.rem(b + 1, n_blk)
     own = ball.at[pl.ds(rows, rows)]
 
-    def tile(ref, i, j):
-        return ref.at[
-            pl.ds(pl.multiple_of(i * BS, BS), BS), pl.ds(pl.multiple_of(j * BS, BS), BS)
-        ]
-
     barrier = pltpu.get_barrier_semaphore()
 
     def greet_blk(i, carry):
@@ -76,31 +71,20 @@
     for load in loads:
         load.start()
 
-    def stored(ref, m, v):
-        return ref.at[pl.ds((5 * m + v) * BS, BS)]
-
-    for m in range(2):
-        for c in range(4):
-            pltpu.make_async_copy(
-                stored(dvirt_ref, m, c + 1 - m), tile(dmat, 3 + m, c), load_sem.at[1]
-            ).start()
-        pltpu.make_async_copy(stored(dvirt_ref, m, 4 * m), corner.at[m], load_sem.at[1]).start()
-        for v in range(5):
-            pltpu.make_async_copy(
-                stored(docc_ref, m, v), tile(omat, m, m + v), load_sem.at[2]
-            ).start()
-
     greet_blk(1, 0)
     greet_blk(n_blk - 1, 0)
     lax.fori_loop(1, n_aux, greet_aux, 0)
 
-    zero = jnp.zeros((BS, BS), jnp.bfloat16)
-    for c in range(4):
-        for r in range(8):
-            if not 0 <= r - c <= 4:
-                tile(dmat, r, c)[...] = zero
-    for m in range(2):
-        tile(omat, m, 5 - 5 * m)[...] = zero
+    prepare = [
+        pltpu.make_async_copy(dvirt_ref.at[0, pl.ds(1, 4)], dmat.at[3], load_sem.at[1]),
+        pltpu.make_async_copy(dvirt_ref.at[1, pl.ds(0, 4)], dmat.at[4], load_sem.at[1]),
+        pltpu.make_async_copy(dvirt_ref.at[0, 0], corner.at[0], load_sem.at[1]),
+        pltpu.make_async_copy(dvirt_ref.at[1, 4], corner.at[1], load_sem.at[1]),
+        pltpu.make_async_copy(docc_ref.at[0], omat.at[0, pl.ds(0, 5)], load_sem.at[2]),
+        pltpu.make_async_copy(docc_ref.at[1], omat.at[1, pl.ds(1, 5)], load_sem.at[2]),
+    ]
+    for load in prepare:
+        load.start()
 
     for load in loads:
         load.wait()
@@ -124,12 +108,8 @@
     def turn(block):
         return block[...].astype(jnp.float32).T.astype(jnp.bfloat16)
 
-    tile(dmat, 1, 1)[...] = turn(corner.at[0])
-    tile(dmat, 2, 1)[...] = turn(tile(dmat, 3, 0))
-    tile(dmat, 5, 1)[...] = turn(tile(dmat, 3, 3))
-    tile(dmat, 2, 2)[...] = turn(tile(dmat, 4, 0))
-    tile(dmat, 5, 2)[...] = turn(tile(dmat, 4, 3))
-    tile(dmat, 6, 2)[...] = turn(corner.at[1])
+    dmat[5, 1] = turn(dmat.at[3, 3])
+    dmat[2, 2] = turn(dmat.at[4, 0])
     pl.semaphore_wait(barrier, 2 + n_aux - 1)
 
     def tell(step):
@@ -157,7 +137,7 @@
         )
 
     def band(r, c):
-        return dmat.at[pl.ds(r * BS, 3 * BS), pl.ds(c * BS, BS)]
+        return dmat.at[pl.ds(r, 3), c]
 
     rims = [
         to_blk(band(2, 2), band(0, 0), 0, right),
@@ -195,6 +175,18 @@
 
     scatter(ball, rows, all_b, 0)
 
+    dmat[1, 1] = turn(corner.at[0])
+    dmat[2, 1] = turn(dmat.at[3, 0])
+    dmat[5, 2] = turn(dmat.at[4, 3])
+    dmat[6, 2] = turn(corner.at[1])
+    zero = jnp.zeros((BS, BS), jnp.bfloat16)
+    for c in range(4):
+        for r in range(8):
+            if not 0 <= r - c <= 4:
+                dmat[r, c] = zero
+    for m in range(2):
+        omat[m, 5 - 5 * m] = zero
+
     learn(0)
     tell(1)
 
@@ -204,19 +196,16 @@
     learn(1)
     tell(2)
 
+    def grid(blocks):
+        return jnp.concatenate([jnp.concatenate(row, axis=1) for row in blocks], axis=0)
+
     def part(pair):
         blocks = [ball[pl.ds((6 * pair + i) * BS, BS), :] for i in range(6)]
-        b_pair = jnp.concatenate(
-            [
-                jnp.concatenate(blocks[:3] + [zero], axis=1),
-                jnp.concatenate([zero] + blocks[3:], axis=1),
-            ],
-            axis=0,
-        )
-        at = pl.ds(2 * pair * BS, 4 * BS)
-        x_pair = jnp.dot(b_pair, dmat[at, :], preferred_element_type=jnp.float32)
+        b_pair = grid([blocks[:3] + [zero], [zero] + blocks[3:]])
+        d_pair = grid([[dmat[2 * pair + r, c] for c in range(4)] for r in range(4)])
+        x_pair = jnp.dot(b_pair, d_pair, preferred_element_type=jnp.float32)
         return jnp.dot(
-            omat[:, pl.ds(2 * pair * BS, 2 * BS)],
+            grid([[omat[m, 2 * pair + n] for n in range(2)] for m in range(2)]),
             x_pair.astype(jnp.bfloat16),
             preferred_element_type=jnp.float32,
         )
@@ -269,18 +258,22 @@
         row_out[p] = gram[p : p + 1, :]
 
     def send_row(i, carry):
-        there = lax.rem(q + i, n_aux)
-        pltpu.make_async_remote_copy(
-            src_ref=row_out.at[there],
-            dst_ref=row_in.at[q],
-            send_sem=a2a_send.at[2],
-            recv_sem=a2a_recv.at[2],
-            device_id={"aux": there},
-            device_id_type=MESH,
-        ).start()
+        there = lax.rem(i + 1, n_aux)
+
+        @pl.when(there != q)
+        def _():
+            pltpu.make_async_remote_copy(
+                src_ref=row_out.at[there],
+                dst_ref=row_in.at[q],
+                send_sem=a2a_send.at[2],
+                recv_sem=a2a_recv.at[2],
+                device_id={"aux": there},
+                device_id_type=MESH,
+            ).start()
+
         return carry
 
-    lax.fori_loop(1, n_aux, send_row, 0)
+    lax.fori_loop(0, n_aux, send_row, 0)
     row_in[q] = row_out[q]
     scattered(row_in, a2a_recv.at[2])
     sum_out[...] = jnp.sum(row_in[...], axis=0)
@@ -336,8 +329,8 @@
                 pltpu.SMEM(intersection.shape, jnp.int32),
                 pltpu.SMEM(counts.shape, jnp.int32),
                 pltpu.VMEM((rows, BS), jnp.bfloat16),
-                pltpu.VMEM((2 * BS, 6 * BS), jnp.bfloat16),
-                pltpu.VMEM((8 * BS, 4 * BS), jnp.bfloat16),
+                pltpu.VMEM((2, 6, BS, BS), jnp.bfloat16),
+                pltpu.VMEM((8, 4, BS, BS), jnp.bfloat16),
                 pltpu.VMEM((2, BS, BS), jnp.bfloat16),
                 pltpu.VMEM((3 * rows, BS), jnp.bfloat16),
                 pltpu.VMEM((rows, BS), jnp.bfloat16),
@@ -363,8 +356,8 @@
             intersection,
             counts,
             tensor.reshape(rows, BS),
-            d_occ.reshape(2 * 5 * BS, BS),
-            d_virt.reshape(2 * 5 * BS, BS),
+            d_occ,
+            d_virt,
         )
 
     return jax.shard_map(

time: 42.4 us -> 42.3 us (level)
  no operation moved by 1% of the time
where the time goes in v3:
time: 42.3 us; the launch traced here: 42.2 us
  Pallas kernels  41 us (97%)
  local copies, waits for them, and re-layouts  1.19 us (3%)
    pallas_call x1, Pallas kernels, on_device(): pl.pallas_call(functools.partial(kernel, n_blk, n_aux), out_shape=jax.Sha...  41 us
    unnamed x1, local copies, waits for them, and re-layouts  1.19 us

profile of v3, /device:TPU:1, one launch (start us, length us, event | category | flops | bytes accessed | tf_op | source)
XLA Modules:
  0.0 42.2 jit_solution(9939886361533584316)
XLA Ops:
  0.0 41.0 %shard_map.55 = f32[1,16]{1,0:T(1,128)} custom-call(s32[2,2]{1,0:T(2,128)} %inter_hbm.1, s32[64]{0:T(128)} %counts_hbm.1, bf16[768,128]{1,0:T(8,128)(2,1)} %bitcast.1, bf16[2,5,128,128]{3,2,1,0:T(8,128)(2,1)} %docc_ref.1, bf16[2,5,128,128]{3,2,1,0:T(8,128)(2,1)} %dvirt_ref.1), custom_call_target="tpu_custom_call" | custom-call | tf_op jit(solution)/shard_map/pallas_call | solution.py:323
  41.0 1.2 %copy.7 = f32[1,16]{1,0:T(1,128)} copy(f32[1,16]{1,0:T(1,128)} %shard_map.55) | data formatting | bytes 128

commit v4 on v3

--- a/solution.py
+++ b/solution.py
@@ -47,21 +47,14 @@
     nblocks = counts_ref.shape[0]
     rows = raw.shape[0]
     share = rows // n_aux
-    left = lax.rem(b + n_blk - 1, n_blk)
-    right = lax.rem(b + 1, n_blk)
+    left = (b - 1) & (n_blk - 1)
+    right = (b + 1) & (n_blk - 1)
     own = ball.at[pl.ds(rows, rows)]
 
     barrier = pltpu.get_barrier_semaphore()
 
-    def greet_blk(i, carry):
-        there = lax.rem(b + i, n_blk)
-        pl.semaphore_signal(barrier, inc=1, device_id={"blk": there}, device_id_type=MESH)
-        return carry
-
-    def greet_aux(i, carry):
-        there = lax.rem(q + i, n_aux)
-        pl.semaphore_signal(barrier, inc=1, device_id={"aux": there}, device_id_type=MESH)
-        return carry
+    def greet(axis, there):
+        pl.semaphore_signal(barrier, inc=1, device_id={axis: there}, device_id_type=MESH)
 
     loads = [
         pltpu.make_async_copy(tensor_ref, raw, load_sem.at[0]),
@@ -71,9 +64,10 @@
     for load in loads:
         load.start()
 
-    greet_blk(1, 0)
-    greet_blk(n_blk - 1, 0)
-    lax.fori_loop(1, n_aux, greet_aux, 0)
+    greet("blk", right)
+    greet("blk", left)
+    for i in range(1, n_aux):
+        greet("aux", q ^ i)
 
     prepare = [
         pltpu.make_async_copy(dvirt_ref.at[0, pl.ds(1, 4)], dmat.at[3], load_sem.at[1]),
@@ -114,11 +108,11 @@
 
     def tell(step):
         if step < known.shape[0]:
-            for there in (b + 2**step, b + n_blk - 2**step):
+            for there in (b + 2**step, b - 2**step):
                 pl.semaphore_signal(
                     known.at[step],
                     inc=1,
-                    device_id={"blk": lax.rem(there, n_blk)},
+                    device_id={"blk": there & (n_blk - 1)},
                     device_id_type=MESH,
                 )
 
@@ -153,8 +147,8 @@
         def piece(there):
             return src.at[pl.ds(pl.multiple_of(first + there * share, PACK), share)]
 
-        def send(i, carry):
-            there = lax.rem(q + i, n_aux)
+        for i in range(1, n_aux):
+            there = q ^ i
             pltpu.make_async_remote_copy(
                 src_ref=piece(there),
                 dst_ref=dst.at[q],
@@ -163,9 +157,6 @@
                 device_id={"aux": there},
                 device_id_type=MESH,
             ).start()
-            return carry
-
-        lax.fori_loop(1, n_aux, send, 0)
         dst[q] = piece(q)[...]
 
     def scattered(dst, sem):
@@ -257,45 +248,29 @@
     for p in range(n_aux):
         row_out[p] = gram[p : p + 1, :]
 
-    def send_row(i, carry):
-        there = lax.rem(i + 1, n_aux)
-
-        @pl.when(there != q)
-        def _():
-            pltpu.make_async_remote_copy(
-                src_ref=row_out.at[there],
-                dst_ref=row_in.at[q],
-                send_sem=a2a_send.at[2],
-                recv_sem=a2a_recv.at[2],
-                device_id={"aux": there},
-                device_id_type=MESH,
-            ).start()
-
-        return carry
-
-    lax.fori_loop(0, n_aux, send_row, 0)
+    for i in range(1, n_aux):
+        pltpu.make_async_remote_copy(
+            src_ref=row_out.at[q ^ i],
+            dst_ref=row_in.at[q],
+            send_sem=a2a_send.at[2],
+            recv_sem=a2a_recv.at[2],
+            device_id={"aux": q ^ i},
+            device_id_type=MESH,
+        ).start()
     row_in[q] = row_out[q]
     scattered(row_in, a2a_recv.at[2])
     sum_out[...] = jnp.sum(row_in[...], axis=0)
     learn(3)
 
-    def send_sum(i, carry):
-        there = lax.rem(i, 2) * (n_blk // 2) + i // 2
-
-        @pl.when(there != b)
-        def _():
-            pltpu.make_async_remote_copy(
-                src_ref=sum_out,
-                dst_ref=sum_in.at[b],
-                send_sem=a2a_send.at[3],
-                recv_sem=a2a_recv.at[3],
-                device_id={"blk": there},
-                device_id_type=MESH,
-            ).start()
-
-        return carry
-
-    lax.fori_loop(0, n_blk, send_sum, 0)
+    for i in range(n_blk - 1, 0, -1):
+        pltpu.make_async_remote_copy(
+            src_ref=sum_out,
+            dst_ref=sum_in.at[b],
+            send_sem=a2a_send.at[3],
+            recv_sem=a2a_recv.at[3],
+            device_id={"blk": b ^ i},
+            device_id_type=MESH,
+        ).start()
     sum_in[b] = sum_out[...]
     pltpu.make_async_copy(
         sum_in.at[pl.ds(0, n_blk - 1)], sum_in.at[pl.ds(0, n_blk - 1)], a2a_recv.at[3]
@@ -350,7 +325,7 @@
             compiler_params=pltpu.CompilerParams(
                 collective_id=0,
                 has_side_effects=True,
-                vmem_limit_bytes=65536 * 1000,
+                vmem_limit_bytes=56550000,
             ),
         )(
             intersection,

time: 42.3 us -> 41 us (0.969)
  local copies, waits for them, and re-layouts: 1.19 us -> 0.51 us
  Pallas kernels: 41 us -> 40.4 us
    unnamed x1, local copies, waits for them, and re-layouts: 1.19 us -> 0.51 us
    pallas_call x1, Pallas kernels: 41 us -> 40.4 us  [on_device(): pl.pallas_call(functools.partial(kernel, n_blk, n_aux), out_shape=jax.Sha...]
where the time goes in v4:
time: 41 us; the launch traced here: 40.9 us
  Pallas kernels  40.4 us (99%)
  local copies, waits for them, and re-layouts  0.51 us (1%)
    pallas_call x1, Pallas kernels, on_device(): pl.pallas_call(functools.partial(kernel, n_blk, n_aux), out_shape=jax.Sha...  40.4 us

profile of v4, /device:TPU:1, one launch (start us, length us, event | category | flops | bytes accessed | tf_op | source)
XLA Modules:
  0.0 40.9 jit_solution(1563665001483757271)
XLA Ops:
  0.0 40.4 %shard_map.55 = f32[1,16]{1,0:T(1,128)S(1)} custom-call(s32[2,2]{1,0:T(2,128)} %inter_hbm.1, s32[64]{0:T(128)} %counts_hbm.1, bf16[768,128]{1,0:T(8,128)(2,1)} %bitcast.1, bf16[2,5,128,128]{3,2,1,0:T(8,128)(2,1)} %docc_ref.1, bf16[2,5,128,128]{3,2,1,0:T(8,128)(2,1)} %dvirt_ref.1), custom_call_target="tpu_custom_call" | custom-call | tf_op jit(solution)/shard_map/pallas_call | solution.py:298
  40.4 0.5 %copy.7 = f32[1,16]{1,0:T(1,128)} copy(f32[1,16]{1,0:T(1,128)S(1)} %shard_map.55) | data formatting | bytes 128

commit v5 on v4

--- a/solution.py
+++ b/solution.py
@@ -44,6 +44,7 @@
 ):
     b = lax.axis_index("blk")
     q = lax.axis_index("aux")
+    core = q & 1
     nblocks = counts_ref.shape[0]
     rows = raw.shape[0]
     share = rows // n_aux
@@ -139,16 +140,26 @@
         to_blk(own, ball.at[pl.ds(0, rows)], 2, right),
         to_blk(own, ball.at[pl.ds(2 * rows, rows)], 3, left),
     ]
-    for rim in rims:
-        rim.start()
+
+    def leave(order):
+        for k in order:
+            rims[k].start()
+
+    pl.when(core == 0)(functools.partial(leave, (0, 1, 2, 3)))
+    pl.when(core == 1)(functools.partial(leave, (1, 0, 3, 2)))
     tell(0)
+
+    cross = n_aux // 2
+    across_and_along = [cross]
+    for i in list(range(2, cross, 2)) + list(range(1, cross, 2)):
+        across_and_along += [i, cross + i]
 
     def scatter(src, first, dst, sem):
         def piece(there):
             return src.at[pl.ds(pl.multiple_of(first + there * share, PACK), share)]
 
-        for i in range(1, n_aux):
-            there = q ^ i
+        for i in across_and_along:
+            there = q ^ i if i == cross else q ^ i ^ (core * cross)
             pltpu.make_async_remote_copy(
                 src_ref=piece(there),
                 dst_ref=dst.at[q],
@@ -191,7 +202,9 @@
         return jnp.concatenate([jnp.concatenate(row, axis=1) for row in blocks], axis=0)
 
     def part(pair):
-        blocks = [ball[pl.ds((6 * pair + i) * BS, BS), :] for i in range(6)]
+        blocks = [
+            ball[pl.ds(pl.multiple_of((6 * pair + i) * BS, BS), BS), :] for i in range(6)
+        ]
         b_pair = grid([blocks[:3] + [zero], [zero] + blocks[3:]])
         d_pair = grid([[dmat[2 * pair + r, c] for c in range(4)] for r in range(4)])
         x_pair = jnp.dot(b_pair, d_pair, preferred_element_type=jnp.float32)
@@ -202,12 +215,14 @@
         )
 
     total = part(1)
-    rims[2].wait_recv()
-    total = total + part(0)
-    rims[3].wait_recv()
+    pl.when(core == 0)(rims[2].wait_recv)
+    pl.when(core == 1)(rims[3].wait_recv)
+    total = total + part(2 * core)
+    pl.when(core == 1)(rims[2].wait_recv)
+    pl.when(core == 0)(rims[3].wait_recv)
     learn(2)
     tell(3)
-    total = total + part(2)
+    total = total + part(2 - 2 * core)
     total = total.astype(jnp.bfloat16)
     for m in range(2):
         for w in range(3):

time: 41 us -> 41.1 us (level)
  no operation moved by 1% of the time
where the time goes in v5:
time: 41.1 us; the launch traced here: 40.9 us
  Pallas kernels  40.4 us (98%)
  local copies, waits for them, and re-layouts  0.51 us (1%)
    pallas_call x1, Pallas kernels, on_device(): pl.pallas_call(functools.partial(kernel, n_blk, n_aux), out_shape=jax.Sha...  40.4 us

profile of v5, /device:TPU:1, one launch (start us, length us, event | category | flops | bytes accessed | tf_op | source)
XLA Modules:
  0.0 40.9 jit_solution(11170825577789576818)
XLA Ops:
  0.0 40.4 %shard_map.55 = f32[1,16]{1,0:T(1,128)S(1)} custom-call(s32[2,2]{1,0:T(2,128)} %inter_hbm.1, s32[64]{0:T(128)} %counts_hbm.1, bf16[768,128]{1,0:T(8,128)(2,1)} %bitcast.1, bf16[2,5,128,128]{3,2,1,0:T(8,128)(2,1)} %docc_ref.1, bf16[2,5,128,128]{3,2,1,0:T(8,128)(2,1)} %dvirt_ref.1), custom_call_target="tpu_custom_call" | custom-call | tf_op jit(solution)/shard_map/pallas_call | solution.py:313
  40.4 0.5 %copy.7 = f32[1,16]{1,0:T(1,128)} copy(f32[1,16]{1,0:T(1,128)S(1)} %shard_map.55) | data formatting | bytes 128

commit v6 on v4

--- a/solution.py
+++ b/solution.py
@@ -10,6 +10,7 @@
 MESH = pl.DeviceIdType.MESH
 BS = 128
 PACK = 16
+TEAM = 2
 
 
 def kernel(
@@ -41,9 +42,12 @@
     a2a_send,
     a2a_recv,
     known,
+    hand_send,
+    hand_recv,
 ):
     b = lax.axis_index("blk")
     q = lax.axis_index("aux")
+    seat = q & (TEAM - 1)
     nblocks = counts_ref.shape[0]
     rows = raw.shape[0]
     share = rows // n_aux
@@ -131,7 +135,8 @@
         )
 
     def band(r, c):
-        return dmat.at[pl.ds(r, 3), c]
+        strip = BS // TEAM
+        return dmat.at[pl.ds(r, 3), c, pl.ds(pl.multiple_of(seat * strip, PACK), strip)]
 
     rims = [
         to_blk(band(2, 2), band(0, 0), 0, right),
@@ -164,7 +169,6 @@
             dst.at[pl.ds(0, n_aux - 1)], dst.at[pl.ds(0, n_aux - 1)], sem
         ).wait()
 
-    scatter(ball, rows, all_b, 0)
 
     dmat[1, 1] = turn(corner.at[0])
     dmat[2, 1] = turn(dmat.at[3, 0])
@@ -182,10 +186,26 @@
     tell(1)
 
     pltpu.make_async_copy(docc_ref, docc_ref, load_sem.at[2]).wait()
-    rims[0].wait_recv()
-    rims[1].wait_recv()
+    handed = []
+    for side, rim in enumerate((band(0, 0), band(5, 3))):
+        rims[side].wait_recv()
+        for i in range(1, TEAM):
+            handed.append(
+                pltpu.make_async_remote_copy(
+                    src_ref=rim,
+                    dst_ref=rim,
+                    send_sem=hand_send.at[side, i - 1],
+                    recv_sem=hand_recv.at[side, i - 1],
+                    device_id={"aux": q ^ i},
+                    device_id_type=MESH,
+                )
+            )
+            handed[-1].start()
+    scatter(ball, rows, all_b, 0)
     learn(1)
     tell(2)
+    for copy in handed:
+        copy.wait_recv()
 
     def grid(blocks):
         return jnp.concatenate([jnp.concatenate(row, axis=1) for row in blocks], axis=0)
@@ -277,8 +297,8 @@
     ).wait()
     out_ref[...] = jnp.sum(sum_in[...], axis=0)[:, : out_ref.shape[1]]
 
-    for rim in rims:
-        rim.wait_send()
+    for copy in rims + handed:
+        copy.wait_send()
     scattered(all_b, a2a_send.at[0])
     scattered(all_w, a2a_send.at[1])
     scattered(row_in, a2a_send.at[2])
@@ -321,6 +341,8 @@
                 pltpu.SemaphoreType.DMA((5,)),
                 pltpu.SemaphoreType.DMA((5,)),
                 pltpu.SemaphoreType.REGULAR((steps,)),
+                pltpu.SemaphoreType.DMA((2, TEAM - 1)),
+                pltpu.SemaphoreType.DMA((2, TEAM - 1)),
             ],
             compiler_params=pltpu.CompilerParams(
                 collective_id=0,

time: 41 us -> 40.3 us (0.983)
  Pallas kernels: 40.4 us -> 39.6 us
    pallas_call x1, Pallas kernels: 40.4 us -> 39.6 us  [on_device(): pl.pallas_call(functools.partial(kernel, n_blk, n_aux), out_shape=jax.Sha...]
where the time goes in v6:
time: 40.3 us; the launch traced here: 40.2 us
  Pallas kernels  39.6 us (98%)
  local copies, waits for them, and re-layouts  0.51 us (1%)
    pallas_call x1, Pallas kernels, on_device(): pl.pallas_call(functools.partial(kernel, n_blk, n_aux), out_shape=jax.Sha...  39.6 us

profile of v6, /device:TPU:1, one launch (start us, length us, event | category | flops | bytes accessed | tf_op | source)
XLA Modules:
  0.0 40.2 jit_solution(14265511080185692094)
XLA Ops:
  0.0 39.6 %shard_map.55 = f32[1,16]{1,0:T(1,128)S(1)} custom-call(s32[2,2]{1,0:T(2,128)} %inter_hbm.1, s32[64]{0:T(128)} %counts_hbm.1, bf16[768,128]{1,0:T(8,128)(2,1)} %bitcast.1, bf16[2,5,128,128]{3,2,1,0:T(8,128)(2,1)} %docc_ref.1, bf16[2,5,128,128]{3,2,1,0:T(8,128)(2,1)} %dvirt_ref.1), custom_call_target="tpu_custom_call" | custom-call | tf_op jit(solution)/shard_map/pallas_call | solution.py:318
  39.6 0.5 %copy.7 = f32[1,16]{1,0:T(1,128)} copy(f32[1,16]{1,0:T(1,128)S(1)} %shard_map.55) | data formatting | bytes 128

commit v7 on v6

--- a/solution.py
+++ b/solution.py
@@ -11,6 +11,7 @@
 BS = 128
 PACK = 16
 TEAM = 2
+TRANSPOSED = (((1,), (1,)), ((), ()))
 
 
 def kernel(
@@ -50,7 +51,11 @@
     seat = q & (TEAM - 1)
     nblocks = counts_ref.shape[0]
     rows = raw.shape[0]
-    share = rows // n_aux
+    half = n_aux // 2
+    place = q & (half - 1)
+    share = rows // half
+    z = b & (n_blk // 2 - 1)
+    wraps = (z == 0) | (z == n_blk // 2 - 1)
     left = (b - 1) & (n_blk - 1)
     right = (b + 1) & (n_blk - 1)
     own = ball.at[pl.ds(rows, rows)]
@@ -148,27 +153,28 @@
         rim.start()
     tell(0)
 
-    def scatter(src, first, dst, sem):
-        def piece(there):
-            return src.at[pl.ds(pl.multiple_of(first + there * share, PACK), share)]
-
-        for i in range(1, n_aux):
+    def scatter(src, first, dst, slot, sem, partners):
+        for i in partners:
             there = q ^ i
+            at = pl.multiple_of(first + (there & (half - 1)) * share, PACK)
             pltpu.make_async_remote_copy(
-                src_ref=piece(there),
-                dst_ref=dst.at[q],
+                src_ref=src.at[pl.ds(at, share)],
+                dst_ref=dst.at[slot],
                 send_sem=a2a_send.at[sem],
                 recv_sem=a2a_recv.at[sem],
                 device_id={"aux": there},
                 device_id_type=MESH,
             ).start()
-        dst[q] = piece(q)[...]
+
+    def keep_own(src, first, dst, slot):
+        dst[slot] = src[pl.ds(pl.multiple_of(first + place * share, PACK), share), :]
 
     def scattered(dst, sem):
-        pltpu.make_async_copy(
-            dst.at[pl.ds(0, n_aux - 1)], dst.at[pl.ds(0, n_aux - 1)], sem
-        ).wait()
-
+        others = dst.at[pl.ds(0, dst.shape[0] - 1)]
+        pltpu.make_async_copy(others, others, sem).wait()
+
+    def scatter_tensor(partners):
+        scatter(ball, rows, all_b, q, 0, partners)
 
     dmat[1, 1] = turn(corner.at[0])
     dmat[2, 1] = turn(dmat.at[3, 0])
@@ -201,7 +207,9 @@
                 )
             )
             handed[-1].start()
-    scatter(ball, rows, all_b, 0)
+    scatter_tensor(range(1, half))
+    pl.when(jnp.logical_not(wraps))(lambda: scatter_tensor(range(half, n_aux)))
+    keep_own(ball, rows, all_b, q)
     learn(1)
     tell(2)
     for copy in handed:
@@ -225,6 +233,7 @@
     rims[2].wait_recv()
     total = total + part(0)
     rims[3].wait_recv()
+    pl.when(wraps)(lambda: scatter_tensor(range(half, n_aux)))
     learn(2)
     tell(3)
     total = total + part(2)
@@ -235,49 +244,50 @@
                 m * BS : (m + 1) * BS, (m + w) * BS : (m + w + 1) * BS
             ]
 
-    scatter(w_own, 0, all_w, 1)
-    scattered(all_b, a2a_recv.at[0])
+    scatter(w_own, 0, all_w, place, 1, range(1, half))
+    keep_own(w_own, 0, all_w, place)
     groups = range(share // PACK)
     size = n_aux * PACK
 
     def flat(ref):
         return jnp.concatenate(
-            [ref[:, pl.ds(g * PACK, PACK), :].reshape(size, BS) for g in groups], axis=1
+            [ref[:, pl.ds(g * PACK, PACK), :].reshape(ref.shape[0] * PACK, BS) for g in groups],
+            axis=1,
         )
 
-    b_turned = (
-        jnp.swapaxes(flat(all_b).astype(jnp.float32).reshape(n_aux, PACK, share // PACK * BS), 0, 1)
-        .reshape(size, share // PACK * BS)
-        .T.astype(jnp.bfloat16)
+    fold = (
+        lax.broadcasted_iota(jnp.int32, (size, BS), 0) // PACK
+        == lax.broadcasted_iota(jnp.int32, (size, BS), 1)
+    ).astype(jnp.bfloat16)
+    scattered(all_b, a2a_recv.at[0])
+    scattered(all_w, a2a_recv.at[1])
+    gram = lax.dot_general(
+        flat(all_w), flat(all_b), TRANSPOSED, preferred_element_type=jnp.float32
     )
-    scattered(all_w, a2a_recv.at[1])
-    gram = jnp.dot(flat(all_w), b_turned, preferred_element_type=jnp.float32)
-    same = (lax.broadcasted_iota(jnp.int32, (size, size), 0) & (PACK - 1)) == (
-        lax.broadcasted_iota(jnp.int32, (size, size), 1) // n_aux
+    same = (lax.broadcasted_iota(jnp.int32, gram.shape, 0) & (PACK - 1)) == (
+        lax.broadcasted_iota(jnp.int32, gram.shape, 1) & (PACK - 1)
     )
-    gram = jnp.where(same, gram, 0.0)
-    lanes = min(size, BS)
-    gram = functools.reduce(jnp.add, [gram[:, c : c + lanes] for c in range(0, size, lanes)])
-    gram = jnp.sum(gram.reshape(n_aux, PACK, lanes), axis=1)
-    turn_by = lanes // 2
-    while turn_by >= n_aux:
-        gram = gram + pltpu.roll(gram, turn_by, 1)
-        turn_by //= 2
-    if lanes < BS:
-        gram = jnp.concatenate([gram] * (BS // lanes), axis=1)
-    for p in range(n_aux):
+    gram = jnp.sum(jnp.where(same, gram, 0.0).reshape(half, PACK, size), axis=1)
+    terms = []
+    for _ in range(3):
+        terms.append(gram.astype(jnp.bfloat16))
+        gram = gram - terms[-1].astype(jnp.float32)
+    terms = [
+        jnp.dot(term, fold, preferred_element_type=jnp.float32) for term in reversed(terms)
+    ]
+    gram = terms[0] + terms[1] + terms[2]
+    for p in range(half):
         row_out[p] = gram[p : p + 1, :]
-
-    for i in range(1, n_aux):
+    for i in range(1, half):
         pltpu.make_async_remote_copy(
-            src_ref=row_out.at[q ^ i],
-            dst_ref=row_in.at[q],
+            src_ref=row_out.at[place ^ i],
+            dst_ref=row_in.at[place],
             send_sem=a2a_send.at[2],
             recv_sem=a2a_recv.at[2],
             device_id={"aux": q ^ i},
             device_id_type=MESH,
         ).start()
-    row_in[q] = row_out[q]
+    row_in[place] = row_out[place]
     scattered(row_in, a2a_recv.at[2])
     sum_out[...] = jnp.sum(row_in[...], axis=0)
     learn(3)
@@ -310,7 +320,8 @@
 def solution(mesh):
     n_blk, n_aux = mesh.shape["blk"], mesh.shape["aux"]
     rows = 2 * 3 * BS
-    share = rows // n_aux
+    half = n_aux // 2
+    share = rows // half
     steps = n_blk.bit_length() - 2
     hbm = pl.BlockSpec(memory_space=pltpu.HBM)
 
@@ -330,9 +341,9 @@
                 pltpu.VMEM((3 * rows, BS), jnp.bfloat16),
                 pltpu.VMEM((rows, BS), jnp.bfloat16),
                 pltpu.VMEM((n_aux, share, BS), jnp.bfloat16),
-                pltpu.VMEM((n_aux, share, BS), jnp.bfloat16),
-                pltpu.VMEM((n_aux, 1, BS), jnp.float32),
-                pltpu.VMEM((n_aux, 1, BS), jnp.float32),
+                pltpu.VMEM((half, share, BS), jnp.bfloat16),
+                pltpu.VMEM((half, 1, BS), jnp.float32),
+                pltpu.VMEM((half, 1, BS), jnp.float32),
                 pltpu.VMEM((1, BS), jnp.float32),
                 pltpu.VMEM((n_blk, 1, BS), jnp.float32),
                 pltpu.SemaphoreType.DMA((5,)),

time: 40.3 us -> 39.3 us (0.975)
  Pallas kernels: 39.6 us -> 38.7 us
    pallas_call x1, Pallas kernels: 39.6 us -> 38.7 us  [on_device(): pl.pallas_call(functools.partial(kernel, n_blk, n_aux), out_shape=jax.Sha...]
where the time goes in v7:
time: 39.3 us; the launch traced here: 39.2 us
  Pallas kernels  38.7 us (98%)
  local copies, waits for them, and re-layouts  0.51 us (1%)
    pallas_call x1, Pallas kernels, on_device(): pl.pallas_call(functools.partial(kernel, n_blk, n_aux), out_shape=jax.Sha...  38.7 us

profile of v7, /device:TPU:1, one launch (start us, length us, event | category | flops | bytes accessed | tf_op | source)
XLA Modules:
  0.0 39.2 jit_solution(15946608143782998299)
XLA Ops:
  0.0 38.7 %shard_map.55 = f32[1,16]{1,0:T(1,128)S(1)} custom-call(s32[2,2]{1,0:T(2,128)} %inter_hbm.1, s32[64]{0:T(128)} %counts_hbm.1, bf16[768,128]{1,0:T(8,128)(2,1)} %bitcast.1, bf16[2,5,128,128]{3,2,1,0:T(8,128)(2,1)} %docc_ref.1, bf16[2,5,128,128]{3,2,1,0:T(8,128)(2,1)} %dvirt_ref.1), custom_call_target="tpu_custom_call" | custom-call | tf_op jit(solution)/shard_map/pallas_call | solution.py:329
  38.7 0.5 %copy.7 = f32[1,16]{1,0:T(1,128)} copy(f32[1,16]{1,0:T(1,128)S(1)} %shard_map.55) | data formatting | bytes 128

commit v8 on v7

--- a/solution.py
+++ b/solution.py
@@ -30,6 +30,7 @@
     dmat,
     corner,
     ball,
+    relay,
     w_own,
     all_b,
     all_w,
@@ -45,6 +46,8 @@
     known,
     hand_send,
     hand_recv,
+    relay_send,
+    relay_recv,
 ):
     b = lax.axis_index("blk")
     q = lax.axis_index("aux")
@@ -60,6 +63,13 @@
     right = (b + 1) & (n_blk - 1)
     own = ball.at[pl.ds(rows, rows)]
 
+    n_z = n_blk // 2
+    top = z == n_z - 1
+    across = q ^ half
+    far_side = jnp.where(top, right, left)
+    between = [{"aux": across}, {"blk": b ^ n_z, "aux": across}]
+    beyond = [{"blk": far_side, "aux": across}, {"blk": far_side ^ n_z, "aux": across}]
+
     barrier = pltpu.get_barrier_semaphore()
 
     def greet(axis, there):
@@ -77,6 +87,12 @@
     greet("blk", left)
     for i in range(1, n_aux):
         greet("aux", q ^ i)
+
+    @pl.when(wraps)
+    def _():
+        for there in [between[1]] + beyond:
+            pl.semaphore_signal(barrier, inc=1, device_id=there, device_id_type=MESH)
+
 
     prepare = [
         pltpu.make_async_copy(dvirt_ref.at[0, pl.ds(1, 4)], dmat.at[3], load_sem.at[1]),
@@ -113,7 +129,7 @@
 
     dmat[5, 1] = turn(dmat.at[3, 3])
     dmat[2, 2] = turn(dmat.at[4, 0])
-    pl.semaphore_wait(barrier, 2 + n_aux - 1)
+    pl.semaphore_wait(barrier, 2 + n_aux - 1 + jnp.where(wraps, 3, 0))
 
     def tell(step):
         if step < known.shape[0]:
@@ -149,8 +165,45 @@
         to_blk(own, ball.at[pl.ds(0, rows)], 2, right),
         to_blk(own, ball.at[pl.ds(2 * rows, rows)], 3, left),
     ]
-    for rim in rims:
-        rim.start()
+    rims[0].start()
+    rims[1].start()
+    pl.when(jnp.logical_not(top))(rims[2].start)
+    pl.when(z != 0)(rims[3].start)
+    part_rows = rows // 2
+
+    def pass_on(src, dst, send, recv, there):
+        pltpu.make_async_remote_copy(
+            src_ref=src,
+            dst_ref=dst,
+            send_sem=send,
+            recv_sem=recv,
+            device_id=there,
+            device_id_type=MESH,
+        ).start()
+
+    def outward(side):
+        for k in range(2):
+            pass_on(
+                own.at[pl.ds(k * part_rows, part_rows)],
+                relay.at[k],
+                rim_send.at[side],
+                relay_recv.at[k],
+                between[k],
+            )
+
+    def onward(side):
+        for k in range(2):
+            pltpu.make_async_copy(relay.at[k], relay.at[k], relay_recv.at[k]).wait()
+            pass_on(
+                relay.at[k],
+                ball.at[pl.ds((side - 2) * 2 * rows + k * part_rows, part_rows)],
+                relay_send,
+                rim_recv.at[side],
+                beyond[k],
+            )
+
+    pl.when(top)(functools.partial(outward, 2))
+    pl.when(z == 0)(functools.partial(outward, 3))
     tell(0)
 
     def scatter(src, first, dst, slot, sem, partners):
@@ -210,6 +263,8 @@
     scatter_tensor(range(1, half))
     pl.when(jnp.logical_not(wraps))(lambda: scatter_tensor(range(half, n_aux)))
     keep_own(ball, rows, all_b, q)
+    pl.when(top)(functools.partial(onward, 2))
+    pl.when(z == 0)(functools.partial(onward, 3))
     learn(1)
     tell(2)
     for copy in handed:
@@ -309,6 +364,11 @@
 
     for copy in rims + handed:
         copy.wait_send()
+
+    @pl.when(wraps)
+    def _():
+        pltpu.make_async_copy(relay, relay, relay_send).wait()
+
     scattered(all_b, a2a_send.at[0])
     scattered(all_w, a2a_send.at[1])
     scattered(row_in, a2a_send.at[2])
@@ -339,6 +399,7 @@
                 pltpu.VMEM((8, 4, BS, BS), jnp.bfloat16),
                 pltpu.VMEM((2, BS, BS), jnp.bfloat16),
                 pltpu.VMEM((3 * rows, BS), jnp.bfloat16),
+                pltpu.VMEM((2, rows // 2, BS), jnp.bfloat16),
                 pltpu.VMEM((rows, BS), jnp.bfloat16),
                 pltpu.VMEM((n_aux, share, BS), jnp.bfloat16),
                 pltpu.VMEM((half, share, BS), jnp.bfloat16),
@@ -354,6 +415,8 @@
                 pltpu.SemaphoreType.REGULAR((steps,)),
                 pltpu.SemaphoreType.DMA((2, TEAM - 1)),
                 pltpu.SemaphoreType.DMA((2, TEAM - 1)),
+                pltpu.SemaphoreType.DMA,
+                pltpu.SemaphoreType.DMA((2,)),
             ],
             compiler_params=pltpu.CompilerParams(
                 collective_id=0,

time: 39.3 us -> 40.7 us (1.036)
  Pallas kernels: 38.7 us -> 40 us
    pallas_call x1, Pallas kernels: 38.7 us -> 40 us  [on_device(): pl.pallas_call(functools.partial(kernel, n_blk, n_aux), out_shape=jax.Sha...]
where the time goes in v8:
time: 40.7 us; the launch traced here: 40.6 us
  Pallas kernels  40 us (98%)
  local copies, waits for them, and re-layouts  0.51 us (1%)
    pallas_call x1, Pallas kernels, on_device(): pl.pallas_call(functools.partial(kernel, n_blk, n_aux), out_shape=jax.Sha...  40 us

profile of v8, /device:TPU:1, one launch (start us, length us, event | category | flops | bytes accessed | tf_op | source)
XLA Modules:
  0.0 40.6 jit_solution(17650295145213045661)
XLA Ops:
  0.0 40.0 %shard_map.55 = f32[1,16]{1,0:T(1,128)S(1)} custom-call(s32[2,2]{1,0:T(2,128)} %inter_hbm.1, s32[64]{0:T(128)} %counts_hbm.1, bf16[768,128]{1,0:T(8,128)(2,1)} %bitcast.1, bf16[2,5,128,128]{3,2,1,0:T(8,128)(2,1)} %docc_ref.1, bf16[2,5,128,128]{3,2,1,0:T(8,128)(2,1)} %dvirt_ref.1), custom_call_target="tpu_custom_call" | custom-call | tf_op jit(solution)/shard_map/pallas_call | solution.py:389
  40.1 0.5 %copy.7 = f32[1,16]{1,0:T(1,128)} copy(f32[1,16]{1,0:T(1,128)S(1)} %shard_map.55) | data formatting | bytes 128

commit v9 on v7

--- a/solution.py
+++ b/solution.py
@@ -75,6 +75,8 @@
 
     greet("blk", right)
     greet("blk", left)
+    greet("blk", (b + 2) & (n_blk - 1))
+    greet("blk", (b - 2) & (n_blk - 1))
     for i in range(1, n_aux):
         greet("aux", q ^ i)
 
@@ -113,11 +115,13 @@
 
     dmat[5, 1] = turn(dmat.at[3, 3])
     dmat[2, 2] = turn(dmat.at[4, 0])
-    pl.semaphore_wait(barrier, 2 + n_aux - 1)
+    pl.semaphore_wait(barrier, 4 + n_aux - 1)
+
+    steps = n_blk.bit_length() - 3
 
     def tell(step):
-        if step < known.shape[0]:
-            for there in (b + 2**step, b - 2**step):
+        if step < steps:
+            for there in (b + 2 ** (step + 1), b - 2 ** (step + 1)):
                 pl.semaphore_signal(
                     known.at[step],
                     inc=1,
@@ -126,7 +130,7 @@
                 )
 
     def learn(step):
-        if step < known.shape[0]:
+        if step < steps:
             pl.semaphore_wait(known.at[step], 2)
 
     def to_blk(src, dst, sem, there):
@@ -188,8 +192,6 @@
     for m in range(2):
         omat[m, 5 - 5 * m] = zero
 
-    learn(0)
-    tell(1)
 
     pltpu.make_async_copy(docc_ref, docc_ref, load_sem.at[2]).wait()
     handed = []
@@ -210,8 +212,8 @@
     scatter_tensor(range(1, half))
     pl.when(jnp.logical_not(wraps))(lambda: scatter_tensor(range(half, n_aux)))
     keep_own(ball, rows, all_b, q)
-    learn(1)
-    tell(2)
+    learn(0)
+    tell(1)
     for copy in handed:
         copy.wait_recv()
 
@@ -234,8 +236,6 @@
     total = total + part(0)
     rims[3].wait_recv()
     pl.when(wraps)(lambda: scatter_tensor(range(half, n_aux)))
-    learn(2)
-    tell(3)
     total = total + part(2)
     total = total.astype(jnp.bfloat16)
     for m in range(2):
@@ -246,6 +246,8 @@
 
     scatter(w_own, 0, all_w, place, 1, range(1, half))
     keep_own(w_own, 0, all_w, place)
+    learn(1)
+    tell(2)
     groups = range(share // PACK)
     size = n_aux * PACK
 
@@ -290,7 +292,7 @@
     row_in[place] = row_out[place]
     scattered(row_in, a2a_recv.at[2])
     sum_out[...] = jnp.sum(row_in[...], axis=0)
-    learn(3)
+    learn(2)
 
     for i in range(n_blk - 1, 0, -1):
         pltpu.make_async_remote_copy(
@@ -322,7 +324,7 @@
     rows = 2 * 3 * BS
     half = n_aux // 2
     share = rows // half
-    steps = n_blk.bit_length() - 2
+    steps = max(1, n_blk.bit_length() - 3)
     hbm = pl.BlockSpec(memory_space=pltpu.HBM)
 
     def on_device(tensor, intersection, counts, d_occ, d_virt):

time: 39.3 us -> 39.1 us (level)
  no operation moved by 1% of the time
where the time goes in v9:
time: 39.1 us; the launch traced here: 39 us
  Pallas kernels  38.4 us (98%)
  local copies, waits for them, and re-layouts  0.51 us (1%)
    pallas_call x1, Pallas kernels, on_device(): pl.pallas_call(functools.partial(kernel, n_blk, n_aux), out_shape=jax.Sha...  38.4 us

profile of v9, /device:TPU:1, one launch (start us, length us, event | category | flops | bytes accessed | tf_op | source)
XLA Modules:
  0.0 39.0 jit_solution(14487339518522232213)
XLA Ops:
  0.0 38.4 %shard_map.55 = f32[1,16]{1,0:T(1,128)S(1)} custom-call(s32[2,2]{1,0:T(2,128)} %inter_hbm.1, s32[64]{0:T(128)} %counts_hbm.1, bf16[768,128]{1,0:T(8,128)(2,1)} %bitcast.1, bf16[2,5,128,128]{3,2,1,0:T(8,128)(2,1)} %docc_ref.1, bf16[2,5,128,128]{3,2,1,0:T(8,128)(2,1)} %dvirt_ref.1), custom_call_target="tpu_custom_call" | custom-call | tf_op jit(solution)/shard_map/pallas_call | solution.py:331
  38.4 0.5 %copy.7 = f32[1,16]{1,0:T(1,128)} copy(f32[1,16]{1,0:T(1,128)S(1)} %shard_map.55) | data formatting | bytes 128

commit v10 on v9

--- a/solution.py
+++ b/solution.py
@@ -10,7 +10,7 @@
 MESH = pl.DeviceIdType.MESH
 BS = 128
 PACK = 16
-TEAM = 2
+TEAM = 4
 TRANSPOSED = (((1,), (1,)), ((), ()))
 
 
@@ -225,18 +225,19 @@
         b_pair = grid([blocks[:3] + [zero], [zero] + blocks[3:]])
         d_pair = grid([[dmat[2 * pair + r, c] for c in range(4)] for r in range(4)])
         x_pair = jnp.dot(b_pair, d_pair, preferred_element_type=jnp.float32)
-        return jnp.dot(
-            grid([[omat[m, 2 * pair + n] for n in range(2)] for m in range(2)]),
-            x_pair.astype(jnp.bfloat16),
-            preferred_element_type=jnp.float32,
-        )
-
-    total = part(1)
+        return x_pair.astype(jnp.bfloat16)
+
+    def pull(places, x_rows):
+        o_rows = grid([[omat[m, n] for n in places] for m in range(2)])
+        return jnp.dot(o_rows, x_rows, preferred_element_type=jnp.float32)
+
+    total = pull((2, 3), part(1))
     rims[2].wait_recv()
-    total = total + part(0)
+    x_left = part(0)
     rims[3].wait_recv()
     pl.when(wraps)(lambda: scatter_tensor(range(half, n_aux)))
-    total = total + part(2)
+    x_rim = jnp.concatenate([x_left, part(2)], axis=0)
+    total = total + pull((0, 1, 4, 5), x_rim)
     total = total.astype(jnp.bfloat16)
     for m in range(2):
         for w in range(3):

time: 39.1 us -> 42 us (1.074)
  Pallas kernels: 38.4 us -> 41.4 us
    pallas_call x1, Pallas kernels: 38.4 us -> 41.4 us  [on_device(): pl.pallas_call(functools.partial(kernel, n_blk, n_aux), out_shape=jax.Sha...]
where the time goes in v10:
time: 42 us; the launch traced here: 41.9 us
  Pallas kernels  41.4 us (99%)
  local copies, waits for them, and re-layouts  0.51 us (1%)
    pallas_call x1, Pallas kernels, on_device(): pl.pallas_call(functools.partial(kernel, n_blk, n_aux), out_shape=jax.Sha...  41.4 us

profile of v10, /device:TPU:1, one launch (start us, length us, event | category | flops | bytes accessed | tf_op | source)
XLA Modules:
  0.0 41.9 jit_solution(9251814262996904372)
XLA Ops:
  0.0 41.4 %shard_map.55 = f32[1,16]{1,0:T(1,128)S(1)} custom-call(s32[2,2]{1,0:T(2,128)} %inter_hbm.1, s32[64]{0:T(128)} %counts_hbm.1, bf16[768,128]{1,0:T(8,128)(2,1)} %bitcast.1, bf16[2,5,128,128]{3,2,1,0:T(8,128)(2,1)} %docc_ref.1, bf16[2,5,128,128]{3,2,1,0:T(8,128)(2,1)} %dvirt_ref.1), custom_call_target="tpu_custom_call" | custom-call | tf_op jit(solution)/shard_map/pallas_call | solution.py:332
  41.4 0.5 %copy.7 = f32[1,16]{1,0:T(1,128)} copy(f32[1,16]{1,0:T(1,128)S(1)} %shard_map.55) | data formatting | bytes 128

commit v11 on v9

--- a/solution.py
+++ b/solution.py
@@ -10,7 +10,6 @@
 MESH = pl.DeviceIdType.MESH
 BS = 128
 PACK = 16
-TEAM = 2
 TRANSPOSED = (((1,), (1,)), ((), ()))
 
 
@@ -43,12 +42,9 @@
     a2a_send,
     a2a_recv,
     known,
-    hand_send,
-    hand_recv,
 ):
     b = lax.axis_index("blk")
     q = lax.axis_index("aux")
-    seat = q & (TEAM - 1)
     nblocks = counts_ref.shape[0]
     rows = raw.shape[0]
     half = n_aux // 2
@@ -144,8 +140,7 @@
         )
 
     def band(r, c):
-        strip = BS // TEAM
-        return dmat.at[pl.ds(r, 3), c, pl.ds(pl.multiple_of(seat * strip, PACK), strip)]
+        return dmat.at[pl.ds(r, 3), c]
 
     rims = [
         to_blk(band(2, 2), band(0, 0), 0, right),
@@ -194,28 +189,13 @@
 
 
     pltpu.make_async_copy(docc_ref, docc_ref, load_sem.at[2]).wait()
-    handed = []
-    for side, rim in enumerate((band(0, 0), band(5, 3))):
-        rims[side].wait_recv()
-        for i in range(1, TEAM):
-            handed.append(
-                pltpu.make_async_remote_copy(
-                    src_ref=rim,
-                    dst_ref=rim,
-                    send_sem=hand_send.at[side, i - 1],
-                    recv_sem=hand_recv.at[side, i - 1],
-                    device_id={"aux": q ^ i},
-                    device_id_type=MESH,
-                )
-            )
-            handed[-1].start()
     scatter_tensor(range(1, half))
     pl.when(jnp.logical_not(wraps))(lambda: scatter_tensor(range(half, n_aux)))
     keep_own(ball, rows, all_b, q)
     learn(0)
     tell(1)
-    for copy in handed:
-        copy.wait_recv()
+    rims[0].wait_recv()
+    rims[1].wait_recv()
 
     def grid(blocks):
         return jnp.concatenate([jnp.concatenate(row, axis=1) for row in blocks], axis=0)
@@ -309,7 +289,7 @@
     ).wait()
     out_ref[...] = jnp.sum(sum_in[...], axis=0)[:, : out_ref.shape[1]]
 
-    for copy in rims + handed:
+    for copy in rims:
         copy.wait_send()
     scattered(all_b, a2a_send.at[0])
     scattered(all_w, a2a_send.at[1])
@@ -354,8 +334,6 @@
                 pltpu.SemaphoreType.DMA((5,)),
                 pltpu.SemaphoreType.DMA((5,)),
                 pltpu.SemaphoreType.REGULAR((steps,)),
-                pltpu.SemaphoreType.DMA((2, TEAM - 1)),
-                pltpu.SemaphoreType.DMA((2, TEAM - 1)),
             ],
             compiler_params=pltpu.CompilerParams(
                 collective_id=0,

time: 39.1 us -> 40.1 us (1.026)
  Pallas kernels: 38.4 us -> 39.4 us
    pallas_call x1, Pallas kernels: 38.4 us -> 39.4 us  [on_device(): pl.pallas_call(functools.partial(kernel, n_blk, n_aux), out_shape=jax.Sha...]
where the time goes in v11:
time: 40.1 us; the launch traced here: 40 us
  Pallas kernels  39.4 us (98%)
  local copies, waits for them, and re-layouts  0.51 us (1%)
    pallas_call x1, Pallas kernels, on_device(): pl.pallas_call(functools.partial(kernel, n_blk, n_aux), out_shape=jax.Sha...  39.4 us

profile of v11, /device:TPU:1, one launch (start us, length us, event | category | flops | bytes accessed | tf_op | source)
XLA Modules:
  0.0 40.0 jit_solution(18003498968548833573)
XLA Ops:
  0.0 39.4 %shard_map.55 = f32[1,16]{1,0:T(1,128)S(1)} custom-call(s32[2,2]{1,0:T(2,128)} %inter_hbm.1, s32[64]{0:T(128)} %counts_hbm.1, bf16[768,128]{1,0:T(8,128)(2,1)} %bitcast.1, bf16[2,5,128,128]{3,2,1,0:T(8,128)(2,1)} %docc_ref.1, bf16[2,5,128,128]{3,2,1,0:T(8,128)(2,1)} %dvirt_ref.1), custom_call_target="tpu_custom_call" | custom-call | tf_op jit(solution)/shard_map/pallas_call | solution.py:311
  39.5 0.5 %copy.7 = f32[1,16]{1,0:T(1,128)} copy(f32[1,16]{1,0:T(1,128)S(1)} %shard_map.55) | data formatting | bytes 128

commit v12 on v10

--- a/solution.py
+++ b/solution.py
@@ -10,7 +10,7 @@
 MESH = pl.DeviceIdType.MESH
 BS = 128
 PACK = 16
-TEAM = 4
+TEAM = 2
 TRANSPOSED = (((1,), (1,)), ((), ()))
 
 

time: 42 us -> 39.1 us (0.931)
  Pallas kernels: 41.4 us -> 38.5 us
    pallas_call x1, Pallas kernels: 41.4 us -> 38.5 us  [on_device(): pl.pallas_call(functools.partial(kernel, n_blk, n_aux), out_shape=jax.Sha...]
where the time goes in v12:
time: 39.1 us; the launch traced here: 39 us
  Pallas kernels  38.5 us (98%)
  local copies, waits for them, and re-layouts  0.51 us (1%)
    pallas_call x1, Pallas kernels, on_device(): pl.pallas_call(functools.partial(kernel, n_blk, n_aux), out_shape=jax.Sha...  38.5 us

profile of v12, /device:TPU:1, one launch (start us, length us, event | category | flops | bytes accessed | tf_op | source)
XLA Modules:
  0.0 39.0 jit_solution(10698964247762011198)
XLA Ops:
  0.0 38.5 %shard_map.55 = f32[1,16]{1,0:T(1,128)S(1)} custom-call(s32[2,2]{1,0:T(2,128)} %inter_hbm.1, s32[64]{0:T(128)} %counts_hbm.1, bf16[768,128]{1,0:T(8,128)(2,1)} %bitcast.1, bf16[2,5,128,128]{3,2,1,0:T(8,128)(2,1)} %docc_ref.1, bf16[2,5,128,128]{3,2,1,0:T(8,128)(2,1)} %dvirt_ref.1), custom_call_target="tpu_custom_call" | custom-call | tf_op jit(solution)/shard_map/pallas_call | solution.py:332
  38.5 0.5 %copy.7 = f32[1,16]{1,0:T(1,128)} copy(f32[1,16]{1,0:T(1,128)S(1)} %shard_map.55) | data formatting | bytes 128

commit v13 on v12

--- a/solution.py
+++ b/solution.py
@@ -273,12 +273,14 @@
     gram = jnp.sum(jnp.where(same, gram, 0.0).reshape(half, PACK, size), axis=1)
     terms = []
     for _ in range(3):
-        terms.append(gram.astype(jnp.bfloat16))
-        gram = gram - terms[-1].astype(jnp.float32)
-    terms = [
-        jnp.dot(term, fold, preferred_element_type=jnp.float32) for term in reversed(terms)
-    ]
-    gram = terms[0] + terms[1] + terms[2]
+        terms.append(gram.astype(jnp.bfloat16).astype(jnp.float32))
+        gram = gram - terms[-1]
+    terms = jnp.dot(
+        jnp.concatenate(terms[::-1], axis=0).astype(jnp.bfloat16),
+        fold,
+        preferred_element_type=jnp.float32,
+    )
+    gram = terms[:half] + terms[half : 2 * half] + terms[2 * half :]
     for p in range(half):
         row_out[p] = gram[p : p + 1, :]
     for i in range(1, half):

time: 39.1 us -> 39.1 us (level)
  no operation moved by 1% of the time
where the time goes in v13:
time: 39.1 us; the launch traced here: 39 us
  Pallas kernels  38.5 us (98%)
  local copies, waits for them, and re-layouts  0.51 us (1%)
    pallas_call x1, Pallas kernels, on_device(): pl.pallas_call(functools.partial(kernel, n_blk, n_aux), out_shape=jax.Sha...  38.5 us

profile of v13, /device:TPU:1, one launch (start us, length us, event | category | flops | bytes accessed | tf_op | source)
XLA Modules:
  0.0 39.0 jit_solution(17539861571483213492)
XLA Ops:
  0.0 38.5 %shard_map.55 = f32[1,16]{1,0:T(1,128)S(1)} custom-call(s32[2,2]{1,0:T(2,128)} %inter_hbm.1, s32[64]{0:T(128)} %counts_hbm.1, bf16[768,128]{1,0:T(8,128)(2,1)} %bitcast.1, bf16[2,5,128,128]{3,2,1,0:T(8,128)(2,1)} %docc_ref.1, bf16[2,5,128,128]{3,2,1,0:T(8,128)(2,1)} %dvirt_ref.1), custom_call_target="tpu_custom_call" | custom-call | tf_op jit(solution)/shard_map/pallas_call | solution.py:334
  38.5 0.5 %copy.7 = f32[1,16]{1,0:T(1,128)} copy(f32[1,16]{1,0:T(1,128)S(1)} %shard_map.55) | data formatting | bytes 128
